TPU v7x, 256 devices: a whole 4x4x8 slice. The times are simulated.
256 devices in a mesh: dp: 64 (over z_lo, y, x), mp: 4 (over z_hi, core).
Axes of the slice: x: 4, y: 4, z: 8 (z_hi: 2, z_lo: 4; z = z_hi * 4 + z_lo), core: 2. Of those that a mesh axis runs over, the one named last changes fastest.
Arguments:
- tokens: bfloat16 [16384, 8192], P('dp', 'mp'), may hold values from -8 to 8
- attn_gain: bfloat16 [8192], replicated, may hold values from 0.5 to 1.5
- w_query: bfloat16 [8192, 4096], P('dp', 'mp'), may hold values from -2 to 2
- key_projection_weight: bfloat16 [8192, 512], P('dp', 'mp'), may hold values from -2 to 2
- value_projection_weight: bfloat16 [8192, 512], P('dp', 'mp'), may hold values from -0.0625 to 0.0625
- w_out: bfloat16 [4096, 8192], P('mp', 'dp'), may hold values from -0.09375 to 0.09375
- final_gain: bfloat16 [8192], P('mp'), may hold values from 0.5 to 1.5
- unembed: bfloat16 [64128, 8192], P('dp', 'mp'), may hold values from -0.29882812 to 0.29882812
- clean_ids: int32 [64], replicated, may hold values from 0 to 64127, as said below
- corrupt_ids: int32 [64], replicated, may hold values from 0 to 64127
Outputs:
- head_out: bfloat16 [16384, 4096], P('dp', 'mp')
- scores: float32 [64, 32], P('dp', 'mp')
- metric: float32 [64], P('dp')
Inputs may be any that keep to these rules, and one draw needn't show every extreme that they name: `clean_ids`: split the ids into 64 aligned blocks of equal size and number the groups of 1 sequence alike; the block of a clean answer, minus the number of its sequence's group, taken modulo the number of blocks, is drawn so that every such offset occurs for some sequence.
All inputs are finite; a program needn't handle non-finite values.
Results may differ from a plain program's by a relative error of at most 0.015.
Values may be sent and summed in bfloat16 or wider, within the bound.
No kernel may reach another device: no remote copies, remote signals or barrier semaphores. Data moves between devices by JAX's collectives and lax.ppermute only.
A program may use at most 128 MiB of HBM per device.

v0:
```python
import math
import jax
import jax.numpy as jnp
from jax import lax
from jax.sharding import PartitionSpec as P

MODEL_WIDTH = 8192
HEAD_SIZE = 128
SEQUENCE_LENGTH = 256


def side_by_side(arrays, axis, dim, along):
    ends, at = ([], 0)
    for a in arrays[:-1]:
        at += a.shape[along]
        ends.append(at)
    both = jnp.concatenate(arrays, axis=along)
    return tuple(jnp.split(lax.all_gather(both, axis, axis=dim, tiled=True), ends, axis=along))


def from_everyone(value, axis):
    count = lax.axis_size(axis)
    return lax.all_to_all(
        jnp.broadcast_to(value[None], (count, *value.shape)), axis, 0, 0, tiled=True
    )


def of_everyone(value, axis):
    return from_everyone(value, axis).sum(axis=0)


def joined_along(parts, dim):
    parts = jnp.moveaxis(parts, 0, dim)
    lengths = parts.shape
    return parts.reshape(*lengths[:dim], lengths[dim] * lengths[dim + 1], *lengths[dim + 2 :])


def gather_directly(value, axis, dim):
    return joined_along(from_everyone(value, axis), dim)


def of_everyone_2(value, axis):
    everything = from_everyone(value, axis)
    return jnp.sum(everything.astype(jnp.float32), axis=0)


def cut_along(value, dim, count):
    lengths = value.shape
    parts = value.reshape(*lengths[:dim], count, lengths[dim] // count, *lengths[dim + 1 :])
    return jnp.moveaxis(parts, dim, 0)


def summed_on_arrival(value, axis, dim):
    count = lax.axis_size(axis)
    parts = lax.all_to_all(cut_along(value, dim, count), axis, 0, 0, tiled=True)
    return jnp.sum(parts, axis=0)


def together(arrays, axis):
    ends = [0]
    for a in arrays:
        ends.append(ends[-1] + a.size)
    subtotal = of_everyone(jnp.concatenate([a.ravel() for a in arrays]), axis)
    return tuple((subtotal[b:e].reshape(a.shape) for a, b, e in zip(arrays, ends, ends[1:])))


def apply_rotary(tensor, length):
    half_dim = tensor.shape[-1] // 2
    positions = jnp.arange(length, dtype=jnp.float32)
    inv_freq = jnp.exp(
        jnp.arange(half_dim, dtype=jnp.float32) * (-2.0 * math.log(500000.0) / tensor.shape[-1])
    )
    angles = positions[:, None] * inv_freq[None, :]
    cosine_table = jnp.cos(angles)[:, None, :]
    sine_table = jnp.sin(angles)[:, None, :]
    lower_half = tensor[..., :half_dim]
    upper_half = tensor[..., half_dim:]
    return jnp.concatenate(
        [
            lower_half * cosine_table - upper_half * sine_table,
            upper_half * cosine_table + lower_half * sine_table,
        ],
        axis=-1,
    )


def per_device(
    tokens,
    attn_gain,
    w_query,
    key_projection_weight,
    value_projection_weight,
    w_out,
    final_gain,
    unembed,
    clean_ids,
    corrupt_ids,
):
    row_count = tokens.shape[0]
    seq_count = row_count // SEQUENCE_LENGTH
    gathered = lax.all_gather(tokens, "mp", axis=1, tiled=True)
    wide = gathered.astype(jnp.float32)
    normalized_rows = (
        wide
        * lax.rsqrt(jnp.mean(wide * wide, axis=1, keepdims=True) + 1e-05)
        * attn_gain.astype(jnp.float32)
    ).astype(jnp.bfloat16)
    weight_pieces = side_by_side(
        (w_query, key_projection_weight, value_projection_weight), "dp", 0, 1
    )
    query_raw, key_raw, value_raw = tuple(
        (
            jnp.dot(normalized_rows, weight_piece, preferred_element_type=jnp.float32)
            for weight_piece in weight_pieces
        )
    )
    q_heads = query_raw.shape[1] // HEAD_SIZE
    kv_heads = key_raw.shape[1] // HEAD_SIZE
    query_group_width = q_heads // kv_heads
    queries = apply_rotary(
        query_raw.reshape(seq_count, SEQUENCE_LENGTH, q_heads, HEAD_SIZE), SEQUENCE_LENGTH
    ).astype(jnp.bfloat16)
    projected_key_rows = apply_rotary(
        key_raw.reshape(seq_count, SEQUENCE_LENGTH, kv_heads, HEAD_SIZE), SEQUENCE_LENGTH
    ).astype(jnp.bfloat16)
    value_rows = value_raw.astype(jnp.bfloat16).reshape(
        seq_count, SEQUENCE_LENGTH, kv_heads, HEAD_SIZE
    )
    grouped = queries.reshape(seq_count, SEQUENCE_LENGTH, kv_heads, query_group_width, HEAD_SIZE)
    logits = jnp.einsum(
        "btkgd,bskd->bkgts", grouped, projected_key_rows, preferred_element_type=jnp.float32
    ) / math.sqrt(HEAD_SIZE)
    causal = jnp.arange(SEQUENCE_LENGTH)[:, None] >= jnp.arange(SEQUENCE_LENGTH)[None, :]
    logits = jnp.where(causal, logits, -1e30)
    row_top = jnp.max(logits, axis=-1, keepdims=True)
    exponent = jnp.exp(logits - row_top)
    attn_probs = (exponent / jnp.sum(exponent, axis=-1, keepdims=True)).astype(jnp.bfloat16)
    mixed_heads = jnp.einsum(
        "bkgts,bskd->btkgd", attn_probs, value_rows, preferred_element_type=jnp.float32
    )
    head_out = mixed_heads.astype(jnp.bfloat16).reshape(row_count, q_heads * HEAD_SIZE)
    totals = jnp.sum(head_out.astype(jnp.float32), axis=0)
    all_totals = of_everyone(totals, "dp")
    head_mean = all_totals / (row_count * lax.axis_size("dp"))
    last_out = head_out.reshape(seq_count, SEQUENCE_LENGTH, q_heads * HEAD_SIZE)[
        :, SEQUENCE_LENGTH - 1, :
    ]
    every_last = gather_directly(last_out, "dp", 0)
    partial_out = jnp.dot(every_last, w_out, preferred_element_type=jnp.float32)
    summed_out = of_everyone_2(partial_out.astype(jnp.bfloat16), "mp").astype(jnp.float32)
    moved_out = lax.all_to_all(
        summed_out.astype(jnp.bfloat16), "dp", split_axis=0, concat_axis=1, tiled=True
    )
    span = moved_out.shape[1] // lax.axis_size("mp")
    attn_last = lax.dynamic_slice_in_dim(moved_out, lax.axis_index("mp") * span, span, 1)
    last_tokens = tokens.reshape(seq_count, SEQUENCE_LENGTH, tokens.shape[1])[
        :, SEQUENCE_LENGTH - 1, :
    ].astype(jnp.float32)
    residual = last_tokens + attn_last.astype(jnp.float32)
    vocab_rows = unembed.shape[0]
    id_range = lax.axis_index("dp") * vocab_rows + jnp.arange(vocab_rows, dtype=jnp.int32)
    one_hot = (clean_ids[:, None] == id_range[None, :]).astype(jnp.float32) - (
        corrupt_ids[:, None] == id_range[None, :]
    ).astype(jnp.float32)
    direction = summed_on_arrival(
        jnp.dot(one_hot.astype(jnp.bfloat16), unembed, preferred_element_type=jnp.float32), "dp", 0
    )
    weighted = final_gain.astype(jnp.float32) * direction
    square_part, product_part = together(
        (jnp.sum(residual * residual, axis=1), jnp.sum(residual * weighted, axis=1)), "mp"
    )
    inverse = lax.rsqrt(square_part / MODEL_WIDTH + 1e-05)
    metric = inverse * product_part
    grad_last = (
        weighted * inverse[:, None] - residual * (metric * inverse * inverse / MODEL_WIDTH)[:, None]
    ).astype(jnp.bfloat16)
    grad_full = gather_directly(grad_last, "mp", 1)
    grad_seqs = lax.all_to_all(grad_full, "dp", split_axis=1, concat_axis=0, tiled=True)
    head_grads = summed_on_arrival(
        lax.dot_general(
            grad_seqs, w_out, (((1,), (1,)), ((), ())), preferred_element_type=jnp.float32
        ),
        "dp",
        0,
    )
    mean_gap = head_mean[None, :] - last_out.astype(jnp.float32)
    scores = jnp.sum((mean_gap * head_grads).reshape(seq_count, q_heads, HEAD_SIZE), axis=2)
    return (head_out, scores, metric)


def solution(mesh):
    in_specs = (
        P("dp", "mp"),
        P(),
        P("dp", "mp"),
        P("dp", "mp"),
        P("dp", "mp"),
        P("mp", "dp"),
        P("mp"),
        P("dp", "mp"),
        P(),
        P(),
    )
    out_specs = (P("dp", "mp"), P("dp", "mp"), P("dp"))
    return jax.shard_map(
        per_device, mesh=mesh, in_specs=in_specs, out_specs=out_specs, check_vma=False
    )
```

profile of v0, /device:TPU:2, one launch (start us, length us, event | category | flops | bytes accessed | tf_op | source)
XLA Modules:
  0.0 637.6 jit_solution(4554884628780977542)
XLA Ops:
  8.0 1.7 pad_maximum_fusion
  11.0 68.3 %all-gather.3.cloned.1.call-done = bf16[256,8192]{1,0:T(8,128)(2,1)} async-done(((bf16[256,2048]{1,0:T(8,128)(2,1)}), bf16[256,8192]{1,0:T(8,128)(2,1)}) %all-gather.3.cloned.1.call-update) | async-done | bytes 4194320 | tf_op jit(solution)/shard_map/all_gather | solution.py:101
  79.4 3.1 fusion.2
  82.5 380.6 %all-gather.5.cloned.1.call-done = bf16[8192,1280]{1,0:T(8,128)(2,1)} async-done(((bf16[128,1280]{1,0:T(8,128)(2,1)}), bf16[8192,1280]{1,0:T(8,128)(2,1)}) %all-gather.5.cloned.1.call-update) | async-done | bytes 20971536 | tf_op jit(solution)/shard_map/all_gather | solution.py:18
  463.0 9.4 %fusion.10 = f32[32,8,8,128]{3,1,2,0:T(8,128)S(1)} fusion(bf16[8192,1280]{1,0:T(8,128)(2,1)} %all-gather.5.cloned.1.call-done, bf16[256,8192]{1,0:T(8,128)(2,1)} %all-gather.3.cloned.1.call-done, f32[8192]{0:T(1024)S(1)} %convert_element_type.90, f32[256]{0:T(256)S(1)} %add_rsqrt_fusion), kind=kOutput, calls=%fused_computation.16 | convolution fusion | flops 4303355904 | bytes 22053888 | tf_op jit(solution)/shard_map/dot_general | solution.py:113
  473.0 1.6 copy-done.1
  474.6 3.3 fusion.13
  479.7 4.8 convert_reduce_fusion
  487.6 10.2 %all-to-all-start.2 = ((bf16[64,2,512]{2,1,0:T(2,128)(2,1)}), bf16[64,2,512]{2,1,0:T(2,128)(2,1)S(1)}, u32[]{:S(2)}, u32[]{:S(2)}) async-start(bf16[64,2,512]{2,1,0:T(2,128)(2,1)} %reshape.299), calls=%async_computation.2 | async-start | bytes 262144 | tf_op jit(solution)/shard_map/all_to_all | solution.py:23
  497.8 3.1 convolution_bitcast_fusion
  502.2 5.4 all-to-all-done.2
  507.6 5.5 all-to-all-start.1
  513.4 12.6 %all-to-all-done.1 = f32[64,1,2048]{2,1,0:T(1,128)S(1)} async-done(((f32[64,1,2048]{2,1,0:T(1,128)}), f32[64,1,2048]{2,1,0:T(1,128)S(1)}, u32[]{:S(2)}, u32[]{:S(2)}) %all-to-all-start.1) | async-done | bytes 524320 | tf_op jit(solution)/shard_map/all_to_all | solution.py:55
  526.7 4.9 all-to-all-start.3
  531.9 7.7 %all-to-all-done.3 = bf16[4,64,128]{2,1,0:T(8,128)(2,1)S(1)} async-done(((bf16[4,64,128]{2,1,0:T(8,128)(2,1)}), bf16[4,64,128]{2,1,0:T(8,128)(2,1)S(1)}, u32[]{:S(2)}, u32[]{:S(2)}) %all-to-all-start.3) | async-done | bytes 65568 | tf_op jit(solution)/shard_map/all_to_all | solution.py:23
  540.3 5.9 all-to-all-start.4
  546.3 9.0 %all-to-all-done.4 = bf16[64,1,128]{2,1,0:T(2,128)(2,1)S(1)} async-done(((bf16[64,1,128]{2,1,0:T(2,128)(2,1)}), bf16[64,1,128]{2,1,0:T(2,128)(2,1)S(1)}, u32[]{:S(2)}, u32[]{:S(2)}) %all-to-all-start.4) | async-done | bytes 16416 | tf_op jit(solution)/shard_map/all_to_all | solution.py:151
  558.1 10.0 %all_to_all.69 = f32[4,1,2]{2,1,0:T(1,128)S(1)} all-to-all(f32[4,1,2]{2,1,0:T(1,128)S(1)} %broadcast_in_dim.31), channel_id=1, replica_groups=mesh['dp'=64,'mp'=4] {'mp'}, dimensions={0} | all-to-all | bytes 64 | tf_op jit(solution)/shard_map/all_to_all | solution.py:23
  570.9 10.1 %all_to_all.70 = bf16[4,2,1024]{2,1,0:T(2,128)(2,1)S(1)} all-to-all(bf16[4,2,1024]{2,1,0:T(2,128)(2,1)S(1)} %reshape.301), channel_id=1, replica_groups=mesh['dp'=64,'mp'=4] {'mp'}, dimensions={0} | all-to-all | bytes 32768 | tf_op jit(solution)/shard_map/all_to_all | solution.py:23
  581.0 14.0 %all_to_all.71 = bf16[1,64,128]{2,0,1:T(2,128)(2,1)S(1)} all-to-all(bf16[1,64,128]{2,0,1:T(2,128)(2,1)S(1)} %bitcast.88), channel_id=1, replica_groups=mesh['dp'=64,'mp'=4] {'dp'}, dimensions={1} | all-to-all | bytes 32768 | tf_op jit(solution)/shard_map/all_to_all | solution.py:178
  595.8 5.5 all-to-all-start
  602.5 9.7 %all-to-all-done = f32[64,1,1024]{2,1,0:T(1,128)S(1)} async-done(((f32[64,1,1024]{2,1,0:T(1,128)}), f32[64,1,1024]{2,1,0:T(1,128)S(1)}, u32[]{:S(2)}, u32[]{:S(2)}) %all-to-all-start) | async-done | bytes 262176 | tf_op jit(solution)/shard_map/all_to_all | solution.py:23
  612.3 5.8 all-to-all-start.8
  619.4 9.4 %all-to-all-done.8 = f32[64,1,1024]{2,1,0:T(1,128)S(1)} async-done(((f32[64,1,1024]{2,1,0:T(1,128)}), f32[64,1,1024]{2,1,0:T(1,128)S(1)}, u32[]{:S(2)}, u32[]{:S(2)}) %all-to-all-start.8) | async-done | bytes 262176 | tf_op jit(solution)/shard_map/all_to_all | solution.py:55
  (57 shorter events, 19.0 us)
Async XLA Ops:
  7.2 506.0 %copy-start = (bf16[1024,128]{1,0:T(8,128)(2,1)S(1)}, bf16[1024,128]{1,0:T(8,128)(2,1)}, u32[]{:S(2)}) copy-start(bf16[1024,128]{1,0:T(8,128)(2,1)} %param.15) | copy-start | bytes 786436
  7.2 72.2 %all-gather.3.cloned.1.call-start = ((), (), s32[]{:S(2)}) async-start(), calls=%async_computation.9 | async-start | bytes 5242880 | tf_op jit(solution)/shard_map/all_gather | solution.py:101
  7.9 455.1 %all-gather.5.cloned.1.call-start = ((), (), s32[]{:S(2)}) async-start(), calls=%async_computation.10 | async-start | bytes 21299200 | tf_op jit(solution)/shard_map/all_gather | solution.py:18
  472.4 2.2 copy-start.1
  479.7 18.1 %copy-start.3 = (s32[64]{0:T(128)S(1)}, s32[64]{0:T(128)}, u32[]{:S(2)}) copy-start(s32[64]{0:T(128)} %param.19) | copy-start | bytes 772
  479.7 18.1 %copy-start.4 = (s32[64]{0:T(128)S(1)}, s32[64]{0:T(128)}, u32[]{:S(2)}) copy-start(s32[64]{0:T(128)} %param.18) | copy-start | bytes 772
  487.6 20.0 %all-to-all-start.2 = ((bf16[64,2,512]{2,1,0:T(2,128)(2,1)}), bf16[64,2,512]{2,1,0:T(2,128)(2,1)S(1)}, u32[]{:S(2)}, u32[]{:S(2)}) async-start(bf16[64,2,512]{2,1,0:T(2,128)(2,1)} %reshape.299), calls=%async_computation.2 | async-start | bytes 262144 | tf_op jit(solution)/shard_map/all_to_all | solution.py:23
  497.8 48.5 %copy-start.2 = (bf16[2048]{0:T(1024)(128)(2,1)S(1)}, bf16[2048]{0:T(1024)(128)(2,1)}, u32[]{:S(2)}) copy-start(bf16[2048]{0:T(1024)(128)(2,1)} %param.16) | copy-start | bytes 12292
  507.6 18.5 %all-to-all-start.1 = ((f32[64,1,2048]{2,1,0:T(1,128)}), f32[64,1,2048]{2,1,0:T(1,128)S(1)}, u32[]{:S(2)}, u32[]{:S(2)}) async-start(f32[64,1,2048]{2,1,0:T(1,128)} %copy.63), calls=%async_computation.1 | async-start | bytes 1048576 | tf_op jit(solution)/shard_map/all_to_all | solution.py:55
  526.7 13.0 %all-to-all-start.3 = ((bf16[4,64,128]{2,1,0:T(8,128)(2,1)}), bf16[4,64,128]{2,1,0:T(8,128)(2,1)S(1)}, u32[]{:S(2)}, u32[]{:S(2)}) async-start(bf16[4,64,128]{2,1,0:T(8,128)(2,1)} %broadcast_in_dim.30), calls=%async_computation.3 | async-start | bytes 131072 | tf_op jit(solution)/shard_map/all_to_all | solution.py:23
  540.3 15.0 %all-to-all-start.4 = ((bf16[64,1,128]{2,1,0:T(2,128)(2,1)}), bf16[64,1,128]{2,1,0:T(2,128)(2,1)S(1)}, u32[]{:S(2)}, u32[]{:S(2)}) async-start(bf16[64,1,128]{2,1,0:T(2,128)(2,1)} %copy.64), calls=%async_computation.4 | async-start | bytes 65536 | tf_op jit(solution)/shard_map/all_to_all | solution.py:151
  595.8 16.4 %all-to-all-start = ((f32[64,1,1024]{2,1,0:T(1,128)}), f32[64,1,1024]{2,1,0:T(1,128)S(1)}, u32[]{:S(2)}, u32[]{:S(2)}) async-start(f32[64,1,1024]{2,1,0:T(1,128)} %broadcast_in_dim.27), calls=%async_computation | async-start | bytes 524288 | tf_op jit(solution)/shard_map/all_to_all | solution.py:23
  612.3 16.6 %all-to-all-start.8 = ((f32[64,1,1024]{2,1,0:T(1,128)}), f32[64,1,1024]{2,1,0:T(1,128)S(1)}, u32[]{:S(2)}, u32[]{:S(2)}) async-start(f32[64,1,1024]{2,1,0:T(1,128)} %copy.67), calls=%async_computation.8 | async-start | bytes 524288 | tf_op jit(solution)/shard_map/all_to_all | solution.py:55
Sparse Core Ops, SparseCore 0:
  9.8 69.4 all-gather.2
  81.7 381.2 all-gather.4
where the time goes:
time: 639 us; the launch traced here: 638 us
  waiting for transfers between devices  504 us (79%)
  starting transfers between devices  37.9 us (6%)
  blocking collectives  34.1 us (5%)
  matrix products  21.6 us (3%)
  between operations  16.8 us (3%)
  other arithmetic  13.7 us (2%)
  local copies, waits for them, and re-layouts  9.94 us (2%)
    all_gather x1, waiting for transfers between devices, side_by_side(): lax.all_gather(both, axis, axis=dim, tiled=True)  381 us
    all_gather x1, waiting for transfers between devices, per_device(): gathered = lax.all_gather(tokens, 'mp', axis=1, tiled=True)  68.3 us
    all_to_all x3, waiting for transfers between devices, from_everyone(): lax.all_to_all(jnp.broadcast_to(value[None], (count, *value.shape)), axis...  22.8 us
    all_to_all x2, waiting for transfers between devices, summed_on_arrival(): parts = lax.all_to_all(cut_along(value, dim, count), axis, 0, 0, tiled=True)  22.1 us
    all_to_all x3, starting transfers between devices, from_everyone(): lax.all_to_all(jnp.broadcast_to(value[None], (count, *value.shape)), axis...  20.6 us
    all_to_all x2, blocking collectives, from_everyone(): lax.all_to_all(jnp.broadcast_to(value[None], (count, *value.shape)), axis...  20.1 us
    all_to_all x1, blocking collectives, per_device(): lax.all_to_all(grad_full, 'dp', split_axis=1, concat_axis=0, tiled=True)  14 us
  transfers between devices with their start and end apart: 8, of which 8 were waited for; matrix products, arithmetic and copies ran while one was open for 2% of the time, Pallas kernels for 0%

commit v1 on v0

--- a/solution.py
+++ b/solution.py
@@ -98,7 +98,9 @@
 ):
     row_count = tokens.shape[0]
     seq_count = row_count // SEQUENCE_LENGTH
-    gathered = lax.all_gather(tokens, "mp", axis=1, tiled=True)
+    gathered = jnp.concatenate(
+        lax.all_to_all(jnp.stack([tokens] * lax.axis_size("mp")), "mp", 0, 0), axis=1
+    )
     wide = gathered.astype(jnp.float32)
     normalized_rows = (
         wide

time: 639 us -> 669 us (1.047)
  local copies, waits for them, and re-layouts: 9.94 us -> 52.5 us
  waiting for transfers between devices: 504 us -> 475 us
  starting transfers between devices: 37.9 us -> 45.8 us
    all_to_all x0 -> x1, waiting for transfers between devices: none -> 96.3 us  [per_device(): lax.all_to_all(jnp.stack([tokens] * lax.axis_size('mp')), 'mp', 0, 0)]
    all_gather x1 -> x0, waiting for transfers between devices: 68.3 us -> none  [per_device(): gathered = lax.all_gather(tokens, 'mp', axis=1, tiled=True)]
    all_gather x1, waiting for transfers between devices: 381 us -> 325 us  [side_by_side(): lax.all_gather(both, axis, axis=dim, tiled=True)]
    dot_general x0 -> x2, local copies, waits for them, and re-layouts: none -> 34.8 us  [per_device(): jnp.dot(normalized_rows, weight_piece, preferred_element_type=jnp.float32)]
    convert_element_type x0 -> x2, other arithmetic: none -> 8.86 us  [the longest x1 6.31 us: per_device(): wide = gathered.astype(jnp.float32)]
    all_to_all x0 -> x1, starting transfers between devices: none -> 8.59 us  [per_device(): lax.all_to_all(jnp.stack([tokens] * lax.axis_size('mp')), 'mp', 0, 0)]
  transfers between devices with their start and end apart: 8 -> 8, of which waited for: 8 -> 8; matrix products, arithmetic and copies ran while one was open for 2% -> 4% of each run, Pallas kernels for 0% -> 0%
where the time goes in v1:
time: 669 us; the launch traced here: 667 us
  waiting for transfers between devices  475 us (71%)
  local copies, waits for them, and re-layouts  52.5 us (8%)
  starting transfers between devices  45.8 us (7%)
  blocking collectives  34.1 us (5%)
  matrix products  23.2 us (3%)
  other arithmetic  19.4 us (3%)
  between operations  16.8 us (3%)
    all_gather x1, waiting for transfers between devices, side_by_side(): lax.all_gather(both, axis, axis=dim, tiled=True)  325 us
    all_to_all x1, waiting for transfers between devices, per_device(): lax.all_to_all(jnp.stack([tokens] * lax.axis_size('mp')), 'mp', 0, 0)  96.3 us
    dot_general x2, local copies, waits for them, and re-layouts, per_device(): jnp.dot(normalized_rows, weight_piece, preferred_element_type=jnp.float32)  34.8 us
    all_to_all x3, waiting for transfers between devices, from_everyone(): lax.all_to_all(jnp.broadcast_to(value[None], (count, *value.shape)), axis...  22.8 us
    all_to_all x2, waiting for transfers between devices, summed_on_arrival(): parts = lax.all_to_all(cut_along(value, dim, count), axis, 0, 0, tiled=True)  22.1 us
    all_to_all x2, blocking collectives, from_everyone(): lax.all_to_all(jnp.broadcast_to(value[None], (count, *value.shape)), axis...  20.1 us
    all_to_all x3, starting transfers between devices, from_everyone(): lax.all_to_all(jnp.broadcast_to(value[None], (count, *value.shape)), axis...  19.9 us
    dot_general x2, matrix products, per_device(): jnp.dot(normalized_rows, weight_piece, preferred_element_type=jnp.float32)  14.6 us
  transfers between devices with their start and end apart: 8, of which 8 were waited for; matrix products, arithmetic and copies ran while one was open for 4% of the time, Pallas kernels for 0%

profile of v1, /device:TPU:2, one launch (start us, length us, event | category | flops | bytes accessed | tf_op | source)
XLA Modules:
  0.0 667.1 jit_solution(8106063644781515319)
XLA Ops:
  12.8 8.6 %all-to-all-start = ((bf16[4,256,2048]{2,1,0:T(8,128)(2,1)}), bf16[4,256,2048]{2,1,0:T(8,128)(2,1)}, u32[]{:S(2)}, u32[]{:S(2)}) async-start(bf16[4,256,2048]{2,1,0:T(8,128)(2,1)} %stack.4), calls=%async_computation | async-start | bytes 8388608 | tf_op jit(solution)/shard_map/all_to_all | solution.py:102
  21.7 96.3 %all-to-all-done = bf16[4,256,2048]{2,1,0:T(8,128)(2,1)} async-done(((bf16[4,256,2048]{2,1,0:T(8,128)(2,1)}), bf16[4,256,2048]{2,1,0:T(8,128)(2,1)}, u32[]{:S(2)}, u32[]{:S(2)}) %all-to-all-start) | async-done | bytes 4194336 | tf_op jit(solution)/shard_map/all_to_all | solution.py:102
  118.0 6.2 copy.60
  124.2 6.3 convert_element_type.168
  134.2 325.1 %all-gather.2.cloned.1.call-done = bf16[8192,1280]{1,0:T(8,128)(2,1)} async-done(((bf16[128,1280]{1,0:T(8,128)(2,1)}), bf16[8192,1280]{1,0:T(8,128)(2,1)}) %all-gather.2.cloned.1.call-update) | async-done | bytes 20971536 | tf_op jit(solution)/shard_map/all_gather | solution.py:18
  459.3 13.9 %slice_bitcast_fusion = bf16[1024,8192]{0,1:T(8,128)(2,1)} fusion(bf16[8192,1280]{1,0:T(8,128)(2,1)} %all-gather.2.cloned.1.call-done), kind=kLoop, calls=%fused_computation | loop fusion | bytes 33554432 | tf_op jit(solution)/shard_map/dot_general | solution.py:115
  473.2 20.9 %copy.61 = bf16[1024,8192]{1,0:T(8,128)(2,1)} copy(bf16[1024,8192]{0,1:T(8,128)(2,1)} %slice_bitcast_fusion) | data formatting | bytes 33554432 | tf_op jit(solution)/shard_map/dot_general | solution.py:115
  498.3 10.7 %fusion.12 = f32[1,256,8,128]{1,3,2,0:T(8,128)S(1)} fusion(bf16[8,128,8192]{2,1,0:T(8,128)(2,1)} %bitcast.105, f32[256,1,1,1,8192]{0,4,3,2,1:T(8,128)} %bitcast.106, f32[8192]{0:T(1024)S(1)} %convert_element_type.141, f32[256]{0:T(256)S(1)} %add_rsqrt_fusion), kind=kOutput, calls=%fused_computation.19 | convolution fusion | flops 4301258752 | bytes 26248192 | tf_op jit(solution)/shard_map/dot_general | solution.py:115
  510.0 4.7 convert_reduce_fusion
  517.7 9.9 %all-to-all-start.3 = ((bf16[64,2,512]{2,1,0:T(2,128)(2,1)}), bf16[64,2,512]{2,1,0:T(2,128)(2,1)S(1)}, u32[]{:S(2)}, u32[]{:S(2)}) async-start(bf16[64,2,512]{2,1,0:T(2,128)(2,1)} %reshape.382), calls=%async_computation.3 | async-start | bytes 262144 | tf_op jit(solution)/shard_map/all_to_all | solution.py:23
  532.1 5.4 all-to-all-done.3
  537.4 5.5 all-to-all-start.2
  543.3 12.6 %all-to-all-done.2 = f32[64,1,2048]{2,1,0:T(1,128)S(1)} async-done(((f32[64,1,2048]{2,1,0:T(1,128)}), f32[64,1,2048]{2,1,0:T(1,128)S(1)}, u32[]{:S(2)}, u32[]{:S(2)}) %all-to-all-start.2) | async-done | bytes 524320 | tf_op jit(solution)/shard_map/all_to_all | solution.py:55
  556.6 4.5 all-to-all-start.4
  561.4 7.7 %all-to-all-done.4 = bf16[4,64,128]{2,1,0:T(8,128)(2,1)S(1)} async-done(((bf16[4,64,128]{2,1,0:T(8,128)(2,1)}), bf16[4,64,128]{2,1,0:T(8,128)(2,1)S(1)}, u32[]{:S(2)}, u32[]{:S(2)}) %all-to-all-start.4) | async-done | bytes 65568 | tf_op jit(solution)/shard_map/all_to_all | solution.py:23
  569.7 5.9 all-to-all-start.5
  575.7 9.0 %all-to-all-done.5 = bf16[64,1,128]{2,1,0:T(2,128)(2,1)S(1)} async-done(((bf16[64,1,128]{2,1,0:T(2,128)(2,1)}), bf16[64,1,128]{2,1,0:T(2,128)(2,1)S(1)}, u32[]{:S(2)}, u32[]{:S(2)}) %all-to-all-start.5) | async-done | bytes 16416 | tf_op jit(solution)/shard_map/all_to_all | solution.py:153
  587.5 10.0 %all_to_all.74 = f32[4,1,2]{2,1,0:T(1,128)S(1)} all-to-all(f32[4,1,2]{2,1,0:T(1,128)S(1)} %broadcast_in_dim.31), channel_id=1, replica_groups=mesh['dp'=64,'mp'=4] {'mp'}, dimensions={0} | all-to-all | bytes 64 | tf_op jit(solution)/shard_map/all_to_all | solution.py:23
  600.3 10.1 %all_to_all.75 = bf16[4,2,1024]{2,1,0:T(2,128)(2,1)S(1)} all-to-all(bf16[4,2,1024]{2,1,0:T(2,128)(2,1)S(1)} %reshape.384), channel_id=1, replica_groups=mesh['dp'=64,'mp'=4] {'mp'}, dimensions={0} | all-to-all | bytes 32768 | tf_op jit(solution)/shard_map/all_to_all | solution.py:23
  610.4 14.0 %all_to_all.76 = bf16[1,64,128]{2,0,1:T(2,128)(2,1)S(1)} all-to-all(bf16[1,64,128]{2,0,1:T(2,128)(2,1)S(1)} %bitcast.110), channel_id=1, replica_groups=mesh['dp'=64,'mp'=4] {'dp'}, dimensions={1} | all-to-all | bytes 32768 | tf_op jit(solution)/shard_map/all_to_all | solution.py:180
  625.3 5.5 all-to-all-start.1
  632.0 9.7 %all-to-all-done.1 = f32[64,1,1024]{2,1,0:T(1,128)S(1)} async-done(((f32[64,1,1024]{2,1,0:T(1,128)}), f32[64,1,1024]{2,1,0:T(1,128)S(1)}, u32[]{:S(2)}, u32[]{:S(2)}) %all-to-all-start.1) | async-done | bytes 262176 | tf_op jit(solution)/shard_map/all_to_all | solution.py:23
  641.7 5.8 all-to-all-start.9
  648.9 9.4 %all-to-all-done.9 = f32[64,1,1024]{2,1,0:T(1,128)S(1)} async-done(((f32[64,1,1024]{2,1,0:T(1,128)}), f32[64,1,1024]{2,1,0:T(1,128)S(1)}, u32[]{:S(2)}, u32[]{:S(2)}) %all-to-all-start.9) | async-done | bytes 262176 | tf_op jit(solution)/shard_map/all_to_all | solution.py:55
  (62 shorter events, 32.4 us)
Async XLA Ops:
  7.2 535.9 %copy-start = (bf16[1024,128]{1,0:T(8,128)(2,1)S(1)}, bf16[1024,128]{1,0:T(8,128)(2,1)}, u32[]{:S(2)}) copy-start(bf16[1024,128]{1,0:T(8,128)(2,1)} %param.15) | copy-start | bytes 786436
  7.2 452.1 %all-gather.2.cloned.1.call-start = ((), (), s32[]{:S(2)}) async-start(), calls=%async_computation.10 | async-start | bytes 21299200 | tf_op jit(solution)/shard_map/all_gather | solution.py:18
  12.8 8.6 %copy-start.2 = (bf16[8192]{0:T(1024)(128)(2,1)S(1)}, bf16[8192]{0:T(1024)(128)(2,1)}, u32[]{:S(2)}) copy-start(bf16[8192]{0:T(1024)(128)(2,1)} %param.11) | copy-start | bytes 49156
  12.8 105.3 %all-to-all-start = ((bf16[4,256,2048]{2,1,0:T(8,128)(2,1)}), bf16[4,256,2048]{2,1,0:T(8,128)(2,1)}, u32[]{:S(2)}, u32[]{:S(2)}) async-start(bf16[4,256,2048]{2,1,0:T(8,128)(2,1)} %stack.4), calls=%async_computation | async-start | bytes 8388608 | tf_op jit(solution)/shard_map/all_to_all | solution.py:102
  124.2 6.3 copy-start.1
  510.0 17.7 %copy-start.4 = (s32[64]{0:T(128)S(1)}, s32[64]{0:T(128)}, u32[]{:S(2)}) copy-start(s32[64]{0:T(128)} %param.19) | copy-start | bytes 772
  510.0 17.7 %copy-start.5 = (s32[64]{0:T(128)S(1)}, s32[64]{0:T(128)}, u32[]{:S(2)}) copy-start(s32[64]{0:T(128)} %param.18) | copy-start | bytes 772
  517.7 19.7 %all-to-all-start.3 = ((bf16[64,2,512]{2,1,0:T(2,128)(2,1)}), bf16[64,2,512]{2,1,0:T(2,128)(2,1)S(1)}, u32[]{:S(2)}, u32[]{:S(2)}) async-start(bf16[64,2,512]{2,1,0:T(2,128)(2,1)} %reshape.382), calls=%async_computation.3 | async-start | bytes 262144 | tf_op jit(solution)/shard_map/all_to_all | solution.py:23
  527.6 48.0 %copy-start.3 = (bf16[2048]{0:T(1024)(128)(2,1)S(1)}, bf16[2048]{0:T(1024)(128)(2,1)}, u32[]{:S(2)}) copy-start(bf16[2048]{0:T(1024)(128)(2,1)} %param.16) | copy-start | bytes 12292
  537.4 18.5 %all-to-all-start.2 = ((f32[64,1,2048]{2,1,0:T(1,128)}), f32[64,1,2048]{2,1,0:T(1,128)S(1)}, u32[]{:S(2)}, u32[]{:S(2)}) async-start(f32[64,1,2048]{2,1,0:T(1,128)} %copy.69), calls=%async_computation.2 | async-start | bytes 1048576 | tf_op jit(solution)/shard_map/all_to_all | solution.py:55
  556.6 12.5 %all-to-all-start.4 = ((bf16[4,64,128]{2,1,0:T(8,128)(2,1)}), bf16[4,64,128]{2,1,0:T(8,128)(2,1)S(1)}, u32[]{:S(2)}, u32[]{:S(2)}) async-start(bf16[4,64,128]{2,1,0:T(8,128)(2,1)} %broadcast_in_dim.30), calls=%async_computation.4 | async-start | bytes 131072 | tf_op jit(solution)/shard_map/all_to_all | solution.py:23
  569.7 15.0 %all-to-all-start.5 = ((bf16[64,1,128]{2,1,0:T(2,128)(2,1)}), bf16[64,1,128]{2,1,0:T(2,128)(2,1)S(1)}, u32[]{:S(2)}, u32[]{:S(2)}) async-start(bf16[64,1,128]{2,1,0:T(2,128)(2,1)} %copy.70), calls=%async_computation.5 | async-start | bytes 65536 | tf_op jit(solution)/shard_map/all_to_all | solution.py:153
  625.3 16.4 %all-to-all-start.1 = ((f32[64,1,1024]{2,1,0:T(1,128)}), f32[64,1,1024]{2,1,0:T(1,128)S(1)}, u32[]{:S(2)}, u32[]{:S(2)}) async-start(f32[64,1,1024]{2,1,0:T(1,128)} %broadcast_in_dim.27), calls=%async_computation.1 | async-start | bytes 524288 | tf_op jit(solution)/shard_map/all_to_all | solution.py:23
  641.7 16.6 %all-to-all-start.9 = ((f32[64,1,1024]{2,1,0:T(1,128)}), f32[64,1,1024]{2,1,0:T(1,128)S(1)}, u32[]{:S(2)}, u32[]{:S(2)}) async-start(f32[64,1,1024]{2,1,0:T(1,128)} %copy.73), calls=%async_computation.9 | async-start | bytes 524288 | tf_op jit(solution)/shard_map/all_to_all | solution.py:55
Sparse Core Ops, SparseCore 0:
  10.4 448.8 all-gather.1
